TPU v7x, 128 devices: a whole 4x4x4 slice. The times are simulated.
128 devices in a mesh: row: 8 (over y, x_lo), col: 16 (over x_hi, z, core).
Axes of the slice: x: 4 (x_hi: 2, x_lo: 2; x = x_hi * 2 + x_lo), y: 4, z: 4, core: 2. Of those that a mesh axis runs over, the one named last changes fastest.
Arguments:
- vectors: float32 [512, 32768], P(None, ('row', 'col')), may hold values from -6 to 6
- blocks: float32 [4096, 131072], P(None, ('row', 'col')), may hold values from -0.3 to 0.3
- blk_row: int32 [131072], P(('row', 'col')), may hold values from 0 to 32767, as said below
- blk_col: int32 [131072], P(('row', 'col')), may hold values from 0 to 32767, as said below
- live_counts: int32 [128], P(('row', 'col')), may hold values from 128 to 1024, as said below
Outputs:
- product: float32 [512, 32768], P(None, ('row', 'col'))
Inputs may be any that keep to these rules, and one draw needn't show every extreme that they name: `blk_row`: A slot of the device at row index r and col index c has a block row in [r * size of col * 256, (r + 1) * size of col * 256). `blk_col`: A slot of the device at col index c has a block column k with (k // 256) % (size of col) == c. `live_counts`: some device has all 1024 slots live.
All inputs are finite; a program needn't handle non-finite values.
Results may differ from a plain program's by a relative error of at most 0.0003.
Values sent between devices are 32-bit elements; how exact they have to be, the bound alone decides.
A program may use at most 128 MiB of HBM per device.

v0:
```python
import jax
import jax.numpy as jnp
from jax import lax
from jax.sharding import PartitionSpec as P

B = 64
NV = 8


def body(vectors, blocks, blk_row, blk_col, live_counts):
    strip_len = vectors.shape[1]
    slot_total = blocks.shape[1]
    feature_rows = vectors.shape[0]
    col_size = lax.axis_size("col")
    row_size = lax.axis_size("row")
    row_index = lax.axis_index("row")
    group_size = min(128, slot_total)
    row_local = blk_row - row_index * (col_size * strip_len)
    col_local = blk_col // strip_len // col_size * strip_len + blk_col % strip_len
    live_total = live_counts[0]
    x_cols = lax.all_gather(vectors, "row", axis=1, tiled=True)
    x_rows = lax.all_gather(vectors, "col", axis=1, tiled=True)
    group_count = slot_total // group_size

    def fetch_slots(step_index):
        offset = step_index * group_size
        block_tile = lax.dynamic_slice_in_dim(blocks, offset, group_size, 1).reshape(
            B, B, group_size
        )
        rows_here = lax.dynamic_slice_in_dim(row_local, offset, group_size, 0)
        cols_here = lax.dynamic_slice_in_dim(col_local, offset, group_size, 0)
        live_mask = (offset + jnp.arange(group_size, dtype=jnp.int32) < live_total).astype(
            jnp.float32
        )
        return (block_tile, rows_here, cols_here, live_mask)

    def plain_add(row_total, block_tile, rows_here, cols_here, live_mask):
        source = jnp.take(x_cols, cols_here, axis=1).reshape(B, NV, group_size)
        products = jnp.einsum("ijg,jvg->ivg", block_tile, source, precision=lax.Precision.HIGHEST)
        return row_total.at[:, rows_here].add(
            products.reshape(feature_rows, group_size) * live_mask
        )

    def mirror_add(col_total, block_tile, rows_here, cols_here, live_mask):
        source = jnp.take(x_rows, rows_here, axis=1).reshape(B, NV, group_size)
        products = jnp.einsum("jig,jvg->ivg", block_tile, source, precision=lax.Precision.HIGHEST)
        return col_total.at[:, cols_here].add(
            products.reshape(feature_rows, group_size) * live_mask
        )

    row_start = jnp.zeros((feature_rows, col_size * strip_len), jnp.float32)
    col_start = jnp.zeros((feature_rows, row_size * strip_len), jnp.float32)

    def plain_step(step_index, row_total):
        return plain_add(row_total, *fetch_slots(step_index))

    def mirror_step(step_index, col_total):
        return mirror_add(col_total, *fetch_slots(step_index))

    row_total = lax.fori_loop(0, group_count, plain_step, row_start)
    col_total = lax.fori_loop(0, group_count, mirror_step, col_start)
    row_part = lax.psum_scatter(row_total, "col", scatter_dimension=1, tiled=True)
    col_part = lax.psum_scatter(col_total, "row", scatter_dimension=1, tiled=True)
    return row_part + col_part


def solution(mesh):
    return jax.shard_map(
        body,
        mesh=mesh,
        in_specs=(
            P(None, ("row", "col")),
            P(None, ("row", "col")),
            P(("row", "col")),
            P(("row", "col")),
            P(("row", "col")),
        ),
        out_specs=P(None, ("row", "col")),
        check_vma=False,
    )
```

profile of v0, /device:TPU:0, one launch (start us, length us, event | category | flops | bytes accessed | tf_op | source)
XLA Modules:
  0.0 625.6 jit_solution(629426222414308904)
XLA Ops:
  10.1 92.1 %all-gather.3.cloned.1.call-done = f32[512,2048]{0,1:T(8,128)} async-done(((f32[512,256]{0,1:T(8,128)}), f32[512,2048]{0,1:T(8,128)}) %all-gather.3.cloned.1.call-update) | async-done | bytes 4194320 | tf_op jit(solution)/shard_map/all_gather | solution.py:21
  106.5 217.2 %while.26 = (s32[]{:T(128)}, f32[512,4096]{0,1:T(8,128)}, s32[1024]{0:T(1024)S(1)}, s32[1024]{0:T(1024)S(1)}, f32[512,2048]{0,1:T(8,128)}, /*index=5*/f32[4096,1...) while((s32[]{:T(128)}, f32[512,4096]{0,1:T(8,128)}, ...), condition=%wide.region_2.3_spmd, body=%wide.region_0.2_spmd.sunk | while | flops 50530820 | bytes 15475631 | solution.py:60
  112.5 4.5 copy.40
  117.0 8.3 %convolution_bitcast_fusion.4 = f32[64,8,128]{0,1,2:T(8,128)S(1)} fusion(f32[64,8,128]{0,1,2:T(8,128)S(1)} %copy.39, f32[64,64,128]{1,0,2:T(8,128)} %copy.40), kind=kOutput, calls=%fused_computation.4.clone.1 | convolution fusion | flops 50331648 | bytes 2621440 | tf_op jit(solution)/shard_map/while/body/eval_jaxpr/ijg,jvg->ivg/dot_general | solution.py:39
  125.8 7.9 %scatter_fusion = f32[512,4096]{0,1:T(8,128)} fusion(f32[512,4096]{0,1:T(8,128)} %get-tuple-element.415, s32[128]{0:T(128)S(1)} %compare_select_fusion.8, f32[128,512]{1,0:T(8,128)S(1)} %copy.42), kind=kCustom, calls=%fused_computation.2.clone.1 | custom fusion | flops 65536 | bytes 786944 | tf_op jit(solution)/shard_map/while/body/eval_jaxpr/scatter-add | solution.py:40
  139.7 4.5 copy.40
  144.2 8.3 %convolution_bitcast_fusion.4 = f32[64,8,128]{0,1,2:T(8,128)S(1)} fusion(f32[64,8,128]{0,1,2:T(8,128)S(1)} %copy.39, f32[64,64,128]{1,0,2:T(8,128)} %copy.40), kind=kOutput, calls=%fused_computation.4.clone.1 | convolution fusion | flops 50331648 | bytes 2621440 | tf_op jit(solution)/shard_map/while/body/eval_jaxpr/ijg,jvg->ivg/dot_general | solution.py:39
  153.0 7.9 %scatter_fusion = f32[512,4096]{0,1:T(8,128)} fusion(f32[512,4096]{0,1:T(8,128)} %get-tuple-element.415, s32[128]{0:T(128)S(1)} %compare_select_fusion.8, f32[128,512]{1,0:T(8,128)S(1)} %copy.42), kind=kCustom, calls=%fused_computation.2.clone.1 | custom fusion | flops 65536 | bytes 786944 | tf_op jit(solution)/shard_map/while/body/eval_jaxpr/scatter-add | solution.py:40
  171.3 8.3 %convolution_bitcast_fusion.4 = f32[64,8,128]{0,1,2:T(8,128)S(1)} fusion(f32[64,8,128]{0,1,2:T(8,128)S(1)} %copy.39, f32[64,64,128]{1,0,2:T(8,128)} %copy.40), kind=kOutput, calls=%fused_computation.4.clone.1 | convolution fusion | flops 50331648 | bytes 2621440 | tf_op jit(solution)/shard_map/while/body/eval_jaxpr/ijg,jvg->ivg/dot_general | solution.py:39
  180.1 7.9 %scatter_fusion = f32[512,4096]{0,1:T(8,128)} fusion(f32[512,4096]{0,1:T(8,128)} %get-tuple-element.415, s32[128]{0:T(128)S(1)} %compare_select_fusion.8, f32[128,512]{1,0:T(8,128)S(1)} %copy.42), kind=kCustom, calls=%fused_computation.2.clone.1 | custom fusion | flops 65536 | bytes 786944 | tf_op jit(solution)/shard_map/while/body/eval_jaxpr/scatter-add | solution.py:40
  198.4 8.3 %convolution_bitcast_fusion.4 = f32[64,8,128]{0,1,2:T(8,128)S(1)} fusion(f32[64,8,128]{0,1,2:T(8,128)S(1)} %copy.39, f32[64,64,128]{1,0,2:T(8,128)} %copy.40), kind=kOutput, calls=%fused_computation.4.clone.1 | convolution fusion | flops 50331648 | bytes 2621440 | tf_op jit(solution)/shard_map/while/body/eval_jaxpr/ijg,jvg->ivg/dot_general | solution.py:39
  207.2 7.9 %scatter_fusion = f32[512,4096]{0,1:T(8,128)} fusion(f32[512,4096]{0,1:T(8,128)} %get-tuple-element.415, s32[128]{0:T(128)S(1)} %compare_select_fusion.8, f32[128,512]{1,0:T(8,128)S(1)} %copy.42), kind=kCustom, calls=%fused_computation.2.clone.1 | custom fusion | flops 65536 | bytes 786944 | tf_op jit(solution)/shard_map/while/body/eval_jaxpr/scatter-add | solution.py:40
  225.6 8.3 %convolution_bitcast_fusion.4 = f32[64,8,128]{0,1,2:T(8,128)S(1)} fusion(f32[64,8,128]{0,1,2:T(8,128)S(1)} %copy.39, f32[64,64,128]{1,0,2:T(8,128)} %copy.40), kind=kOutput, calls=%fused_computation.4.clone.1 | convolution fusion | flops 50331648 | bytes 2621440 | tf_op jit(solution)/shard_map/while/body/eval_jaxpr/ijg,jvg->ivg/dot_general | solution.py:39
  234.4 7.9 %scatter_fusion = f32[512,4096]{0,1:T(8,128)} fusion(f32[512,4096]{0,1:T(8,128)} %get-tuple-element.415, s32[128]{0:T(128)S(1)} %compare_select_fusion.8, f32[128,512]{1,0:T(8,128)S(1)} %copy.42), kind=kCustom, calls=%fused_computation.2.clone.1 | custom fusion | flops 65536 | bytes 786944 | tf_op jit(solution)/shard_map/while/body/eval_jaxpr/scatter-add | solution.py:40
  252.7 8.3 %convolution_bitcast_fusion.4 = f32[64,8,128]{0,1,2:T(8,128)S(1)} fusion(f32[64,8,128]{0,1,2:T(8,128)S(1)} %copy.39, f32[64,64,128]{1,0,2:T(8,128)} %copy.40), kind=kOutput, calls=%fused_computation.4.clone.1 | convolution fusion | flops 50331648 | bytes 2621440 | tf_op jit(solution)/shard_map/while/body/eval_jaxpr/ijg,jvg->ivg/dot_general | solution.py:39
  261.5 7.9 %scatter_fusion = f32[512,4096]{0,1:T(8,128)} fusion(f32[512,4096]{0,1:T(8,128)} %get-tuple-element.415, s32[128]{0:T(128)S(1)} %compare_select_fusion.8, f32[128,512]{1,0:T(8,128)S(1)} %copy.42), kind=kCustom, calls=%fused_computation.2.clone.1 | custom fusion | flops 65536 | bytes 786944 | tf_op jit(solution)/shard_map/while/body/eval_jaxpr/scatter-add | solution.py:40
  279.9 8.3 %convolution_bitcast_fusion.4 = f32[64,8,128]{0,1,2:T(8,128)S(1)} fusion(f32[64,8,128]{0,1,2:T(8,128)S(1)} %copy.39, f32[64,64,128]{1,0,2:T(8,128)} %copy.40), kind=kOutput, calls=%fused_computation.4.clone.1 | convolution fusion | flops 50331648 | bytes 2621440 | tf_op jit(solution)/shard_map/while/body/eval_jaxpr/ijg,jvg->ivg/dot_general | solution.py:39
  288.7 7.9 %scatter_fusion = f32[512,4096]{0,1:T(8,128)} fusion(f32[512,4096]{0,1:T(8,128)} %get-tuple-element.415, s32[128]{0:T(128)S(1)} %compare_select_fusion.8, f32[128,512]{1,0:T(8,128)S(1)} %copy.42), kind=kCustom, calls=%fused_computation.2.clone.1 | custom fusion | flops 65536 | bytes 786944 | tf_op jit(solution)/shard_map/while/body/eval_jaxpr/scatter-add | solution.py:40
  307.0 8.3 %convolution_bitcast_fusion.4 = f32[64,8,128]{0,1,2:T(8,128)S(1)} fusion(f32[64,8,128]{0,1,2:T(8,128)S(1)} %copy.39, f32[64,64,128]{1,0,2:T(8,128)} %copy.40), kind=kOutput, calls=%fused_computation.4.clone.1 | convolution fusion | flops 50331648 | bytes 2621440 | tf_op jit(solution)/shard_map/while/body/eval_jaxpr/ijg,jvg->ivg/dot_general | solution.py:39
  315.8 7.9 %scatter_fusion = f32[512,4096]{0,1:T(8,128)} fusion(f32[512,4096]{0,1:T(8,128)} %get-tuple-element.415, s32[128]{0:T(128)S(1)} %compare_select_fusion.8, f32[128,512]{1,0:T(8,128)S(1)} %copy.42), kind=kCustom, calls=%fused_computation.2.clone.1 | custom fusion | flops 65536 | bytes 786944 | tf_op jit(solution)/shard_map/while/body/eval_jaxpr/scatter-add | solution.py:40
  323.7 8.9 %copy.25 = f32[512,4096]{1,0:T(8,128)} copy(f32[512,4096]{0,1:T(8,128)} %get-tuple-element.253) | data formatting | bytes 16777216 | tf_op jit(solution)/shard_map/while | solution.py:60
  335.3 184.2 %while.27 = (s32[]{:T(128)}, f32[512,2048]{0,1:T(8,128)}, s32[1024]{0:T(1024)S(1)}, s32[1024]{0:T(1024)S(1)}, f32[512,4096]{0,1:T(8,128)}, /*index=5*/f32[4096,1...) while((s32[]{:T(128)}, f32[512,2048]{0,1:T(8,128)}, ...), condition=%wide.region_6.7_spmd, body=%wide.region_4.6_spmd.sunk | while | flops 50530820 | bytes 15475631 | solution.py:61
  342.6 4.5 copy.45
  347.1 5.5 convolution_bitcast_fusion.5
  353.1 5.8 scatter_fusion.1
  366.1 4.5 copy.45
  370.6 5.3 convolution_bitcast_fusion.5
  376.4 5.4 scatter_fusion.1
  389.1 4.5 copy.45
  393.6 5.3 convolution_bitcast_fusion.5
  399.4 5.4 scatter_fusion.1
  412.1 4.5 copy.45
  416.6 5.5 convolution_bitcast_fusion.5
  422.6 5.4 scatter_fusion.1
  435.3 4.5 copy.45
  439.8 5.3 convolution_bitcast_fusion.5
  445.6 5.4 scatter_fusion.1
  458.1 4.5 copy.45
  462.7 5.3 convolution_bitcast_fusion.5
  468.4 5.4 scatter_fusion.1
  481.0 4.5 copy.45
  485.5 5.3 convolution_bitcast_fusion.5
  491.3 5.4 scatter_fusion.1
  503.8 4.5 copy.45
  508.3 5.3 convolution_bitcast_fusion.5
  514.1 5.4 scatter_fusion.1
  519.5 5.5 copy.27
  525.0 91.9 %reduce-scatter.5.cloned.1.call-done = f32[512,256]{1,0:T(8,128)} async-done(((f32[512,2048]{1,0:T(8,128)}), f32[512,256]{1,0:T(8,128)}) %reduce-scatter.5.cloned.1.call-update) | async-done | bytes 524304 | tf_op jit(solution)/shard_map/reduce_scatter | solution.py:63
  (197 shorter events, 151.9 us)
Async XLA Ops:
  6.5 95.7 %all-gather.3.cloned.1.call-start = ((), (), s32[]{:S(2)}) async-start(), calls=%async_computation.2 | async-start | bytes 4718592 | tf_op jit(solution)/shard_map/all_gather | solution.py:21
  8.6 324.3 %all-gather.5.cloned.1.call-start = ((), (), s32[]{:S(2)}) async-start(), calls=%async_computation.4 | async-start | bytes 8912896 | tf_op jit(solution)/shard_map/all_gather | solution.py:22
  9.3 515.7 %reduce-scatter.3.cloned.1.call-start = ((), (), s32[]{:S(2)}) async-start(), calls=%async_computation.3 | async-start | bytes 8912896 | tf_op jit(solution)/shard_map/reduce_scatter | solution.py:62
  332.6 284.4 %reduce-scatter.5.cloned.1.call-start = ((), (), s32[]{:S(2)}) async-start(), calls=%async_computation.5 | async-start | bytes 4718592 | tf_op jit(solution)/shard_map/reduce_scatter | solution.py:63
Sparse Core Ops, SparseCore 0:
  9.0 93.1 all-gather.2
  104.7 73.0 all-gather.4
  332.7 102.8 reduce-scatter.2
  525.1 91.8 reduce-scatter.4
where the time goes:
time: 628 us; the launch traced here: 626 us
  local copies, waits for them, and re-layouts  194 us (31%)
  waiting for transfers between devices  185 us (29%)
  other arithmetic  123 us (20%)
  matrix products  109 us (17%)
  between operations  13.1 us (2%)
    all_gather x1, waiting for transfers between devices, body(): x_cols = lax.all_gather(vectors, 'row', axis=1, tiled=True)  92.1 us
    reduce_scatter x1, waiting for transfers between devices, body(): lax.psum_scatter(col_total, 'row', scatter_dimension=1, tiled=True)  91.9 us
    reshape x16, local copies, waits for them, and re-layouts, fetch_slots(): lax.dynamic_slice_in_dim(blocks, offset, group_size, 1)  72.1 us
    dot_general x8, matrix products, plain_add(): jnp.einsum('ijg,jvg->ivg', block_tile, source, precision=lax.Precision.HI...  66.4 us
    scatter-add x8, other arithmetic, plain_add(): row_total.at[:, rows_here]  63.1 us
    scatter-add x8, other arithmetic, mirror_add(): col_total.at[:, cols_here]  43.7 us
    dot_general x8, matrix products, mirror_add(): jnp.einsum('jig,jvg->ivg', block_tile, source, precision=lax.Precision.HI...  42.7 us
    gather x16, local copies, waits for them, and re-layouts, mirror_add(): source = jnp.take(x_rows, rows_here, axis=1).reshape(B, NV, group_size)  35.3 us
  transfers between devices with their start and end apart: 4, of which 2 were waited for; matrix products, arithmetic and copies ran while one was open for 67% of the time, Pallas kernels for 0%

commit v1 on v0

v1 whole, which is shorter than its diff:
```python
import functools

import jax
import jax.numpy as jnp
from jax import lax
from jax.experimental import pallas as pl
from jax.experimental.pallas import tpu as pltpu
from jax.sharding import PartitionSpec as P

MESH = pl.DeviceIdType.MESH
F32, BF16 = jnp.float32, jnp.bfloat16

B = 64
NV = 8
SB = 256
CAP = 1024
LANES = 128
NROW, NCOL = 8, 16
NZ = 4
HALF = NCOL // 2 * SB
RROWS = NCOL * SB
CROWS = NROW * SB
CHUNKS = 4
VC = NV // CHUNKS
FEAT = VC * B
GROUPS = CAP // LANES
PIECE = 2048
ROWS = RROWS + CROWS
DIRECT = ()

ORDER = (
    "R1.0", "C1.0", "R1.1", "R2.0", "C1.2", "C2.0", "C1.1", "R3a.0", "H.0", "R3b.0", "R2.1",
    "C3a.0", "R1.2", "C3b.0", "R1.3", "C2.2", "R3a.1", "C3a.1", "R4.0", "C2.1", "C1.3", "G1.0",
    "R3b.1", "R5.0", "C3a.2", "R2.2", "C4.0", "G2.0", "V.0", "T.0", "R3a.3", "C3b.1", "S1.0",
    "R3a.2", "R4.1", "C2.3", "R2.3", "G1.1", "S3.0", "S2.0", "R3b.2", "R5.1", "C3b.2", "D2.0",
    "C4.1", "G2.1", "V.1", "R3b.3", "E2b.0", "D3b.0", "T.1", "C3b.3", "R4.2", "E2a.0", "S1.1",
    "S3.1", "G1.2", "S2.1", "R4.3", "C4.2", "E3.0", "R5.2", "D3a.0", "G2.2", "D2.1", "C3a.3",
    "D3.0", "V.2", "D4.0", "E2a.1", "D3b.1", "E4.0", "T.2", "D3a.1", "E2b.1", "G1.3", "F.0", "S1.2",
    "S3.2", "S2.2", "E3.1", "D2.2", "D3.1", "D4.1", "C4.3", "E4.1", "R5.3", "G2.3", "V.3", "E2b.2",
    "T.3", "F.1", "D3b.2", "S1.3", "S2.3", "S3.3", "E3.2", "D2.3", "E2a.2", "D3a.2", "E2b.3",
    "D3a.3", "E2a.3", "D3.2", "D3b.3", "E3.3", "D4.2", "E4.2", "D3.3", "F.2", "E4.3", "D4.3", "F.3",
)


def split(x):
    hi = x.astype(BF16)
    lo = (x - hi.astype(F32)).astype(BF16)
    return jnp.concatenate([hi, lo], axis=0)


def places(rows, cols, live_total):
    here = rows - lax.axis_index("row") * RROWS
    strip = here // SB
    r_place = (strip % 2 * (NCOL // 2) + strip // 2) * SB + here % SB
    c_place = cols // RROWS * SB + cols % SB
    number = lax.broadcasted_iota(jnp.int32, rows.shape, 0) * LANES
    number = number + lax.broadcasted_iota(jnp.int32, rows.shape, 1)
    live = number < live_total
    return jnp.where(live, r_place, -1), jnp.where(live, c_place, -1)


def one_hots(place, first, rows, hot_ref):
    tile = 512

    def step(n, carry):
        start = pl.multiple_of(n * tile, tile)
        number = lax.broadcasted_iota(jnp.int32, (tile, LANES), 0) + start
        for q in range(GROUPS):
            hit = jnp.where(number == place[q : q + 1, :], 1.0, 0.0).astype(BF16)
            hot_ref[pl.ds(first + start, tile), q * LANES : (q + 1) * LANES] = hit
        return carry

    lax.fori_loop(0, rows // tile, step, 0)


def gather(x_ref, c, start, hot_ref):
    rows = pl.ds(pl.multiple_of(start, PIECE), PIECE)
    found = jnp.dot(split(x_ref[c, :, rows]), hot_ref[rows, :], preferred_element_type=F32)
    return found[:FEAT] + found[FEAT:]


def scatter(pt_ref, kind, start, hot_ref, out_ref, b):
    rows = pl.ds(pl.multiple_of(start, PIECE), PIECE)
    total = jnp.dot(hot_ref[rows, :], pt_ref[kind], preferred_element_type=F32)
    out_ref[b, rows, :] = total[:, :FEAT] + total[:, FEAT:]


def multiply(k_ref, g_ref, part_ref):
    tiles = B // 8

    def group(g, carry):
        cols = pl.ds(pl.multiple_of(g * LANES, LANES), LANES)
        x = [
            [g_ref[1, v * B + 8 * t : v * B + 8 * t + 8, cols] for t in range(tiles)]
            for v in range(VC)
        ]

        def rows(i, acc):
            acc = list(acc)
            mirror = [
                g_ref[0, v * B + i * 8 : v * B + i * 8 + 8, cols] for v in range(VC)
            ]
            for u in range(8):
                line = i * 8 + u
                k = [
                    k_ref[g, line * B + 8 * t : line * B + 8 * t + 8, :] for t in range(tiles)
                ]
                for v in range(VC):
                    plain = [k[t] * x[v][t] for t in range(tiles)]
                    while len(plain) > 1:
                        plain = [p + q for p, q in zip(plain[::2], plain[1::2])]
                    part_ref[v, line * 8 : line * 8 + 8, :] = plain[0]
                    other = jnp.broadcast_to(mirror[v][u : u + 1], (8, LANES))
                    for t in range(tiles):
                        acc[v * tiles + t] = acc[v * tiles + t] + k[t] * other
            return acc

        acc = [jnp.zeros((8, LANES), F32) for _ in range(VC * tiles)]
        for i in range(B // 8):
            acc = rows(i, acc)
        for v in range(VC):
            for t in range(tiles):
                here = slice(v * B + 8 * t, v * B + 8 * t + 8)
                g_ref[1, here, cols] = acc[v * tiles + t]
                total = part_ref[v, pl.ds(t * 64, 8, stride=8), :]
                for q in range(1, 8):
                    total = total + part_ref[v, pl.ds(t * 64 + q, 8, stride=8), :]
                g_ref[0, here, cols] = total
        return carry

    lax.fori_loop(0, GROUPS, group, 0)


def kernel(
    vec_ref,
    blk_ref,
    brow_ref,
    bcol_ref,
    live_ref,
    out_ref,
    k_ref,
    x_ref,
    hot_ref,
    p_ref,
    half_ref,
    rb_ref,
    cb_ref,
    g_ref,
    pt_ref,
    part_ref,
    res_ref,
    k_sem,
    v_sem,
    a_send,
    a_row,
    a_col,
    b_send,
    b_row,
    b_col,
    free_sem,
):
    row, col = lax.axis_index("row"), lax.axis_index("col")
    y, xl = row // 2, row % 2
    core, z, xh = col % 2, (col // 2) % NZ, col // 8
    yp, ym, y2 = (y + 1) % NZ, (y + 3) % NZ, (y + 2) % NZ
    zp, zm, z2 = (z + 1) % NZ, (z + 3) % NZ, (z + 2) % NZ

    def at(h, q):
        return (h * NZ + q) * 2 + core

    XH = dict(row=row, col=at(1 - xh, z))
    ZP = dict(row=row, col=at(xh, zp))
    ZM = dict(row=row, col=at(xh, zm))
    Z2 = dict(row=row, col=at(xh, z2))
    SIB = dict(row=row, col=(xh * NZ + z) * 2 + 1 - core)
    XL = dict(row=y * 2 + 1 - xl, col=col)
    YP = dict(row=yp * 2 + xl, col=col)
    YM = dict(row=ym * 2 + xl, col=col)
    Y2 = dict(row=y2 * 2 + xl, col=col)

    def strip(p):
        return pl.ds(pl.multiple_of(p * SB, SB), SB)

    def rstrip(h, q):
        return strip(core * 8 + h * NZ + q)

    def cstrip(q, l):
        return strip(NCOL + q * 2 + l)

    def half(k):
        return pl.ds(pl.multiple_of(k * HALF, HALF), HALF)

    vec_in = [
        pltpu.make_async_copy(
            vec_ref.at[:, h * LANES : (h + 1) * LANES], part_ref.at[h], v_sem.at[h]
        )
        for h in range(2)
    ]
    for load in vec_in:
        load.start()
    loads = [
        pltpu.make_async_copy(
            blk_ref.at[:, g * LANES : (g + 1) * LANES], k_ref.at[g], k_sem.at[g]
        )
        for g in range(GROUPS)
    ]
    for load in loads:
        load.start()

    barrier = pltpu.get_barrier_semaphore()
    for peer in (XH, ZP, ZM, Z2, SIB, XL, YP, YM, Y2):
        pl.semaphore_signal(barrier, inc=1, device_id=peer, device_id_type=MESH)

    for load in vec_in:
        load.wait()
    for c in range(CHUNKS):
        for v in range(VC):
            for h in range(2):
                x = part_ref[h, pl.ds(c * VC + v, B, stride=NV), :]
                for p in (core * 8 + xh * NZ + z, NCOL + row):
                    lanes = pl.ds(pl.multiple_of(p * SB + h * LANES, LANES), LANES)
                    x_ref[c, v * B : (v + 1) * B, lanes] = x

    pl.semaphore_wait(barrier, 9)

    def copy(src, dst, send, recv, peer):
        return pltpu.make_async_remote_copy(
            src_ref=src,
            dst_ref=dst,
            send_sem=send,
            recv_sem=recv,
            device_id=peer,
            device_id_type=MESH,
        )

    def a_r(c, n, h, q, peer):
        part = x_ref.at[c, :, rstrip(h, q)]
        return copy(part, part, a_send.at[c, n], a_row.at[c, h * NZ + q], peer)

    def a_c(c, n, q, l, peer):
        part = x_ref.at[c, :, cstrip(q, l)]
        return copy(part, part, a_send.at[c, n], a_col.at[c, q * 2 + l], peer)

    def a_half(c, k):
        part = x_ref.at[c, :, half(k)]
        return copy(part, part, a_send.at[c, 14], a_row.at[c, 8], SIB)

    def b_r(c, n, h, q, peer):
        src = p_ref.at[c % 2, rstrip(h, q), :]
        return copy(src, rb_ref.at[c, n], b_send.at[c, n], b_row.at[c, n], peer)

    def b_c(c, n, q, l, peer):
        src = p_ref.at[c % 2, cstrip(q, l), :]
        return copy(src, cb_ref.at[c, n], b_send.at[c, 8 + n], b_col.at[c, n], peer)

    def b_half(c):
        src = p_ref.at[c % 2, half(1 - core), :]
        return copy(src, half_ref.at[c % 2], b_send.at[c, 7], b_row.at[c, 7], SIB)

    def add(c, here, arrived, *slots):
        total = p_ref[c % 2, here, :]
        for n in slots:
            total = total + arrived[c, n]
        p_ref[c % 2, here, :] = total

    def out_r(c, n):
        to = (
            (xh, z2, ZP),
            (1 - xh, z2, ZM),
            (1 - xh, zp, ZP),
            (xh, zm, ZM),
            (xh, zp, ZP),
            (1 - xh, zm, ZM),
            (1 - xh, z, XH),
        )
        return b_r(c, n, *to[n])

    def out_c(c, n):
        to = (
            (y2, xl, YP),
            (y2, 1 - xl, YM),
            (yp, 1 - xl, YP),
            (ym, xl, YM),
            (yp, xl, YP),
            (ym, 1 - xl, YM),
            (y, 1 - xl, XL),
        )
        return b_c(c, n, *to[n])

    def H(c):
        r_place, c_place = places(brow_ref[...], bcol_ref[...], live_ref[0])
        one_hots(r_place, 0, RROWS, hot_ref)
        one_hots(c_place, RROWS, CROWS, hot_ref)

    def R1(c):
        a_r(c, 0, xh, z, XH).start()
        a_r(c, 1, xh, z, ZP).start()
        a_r(c, 2, xh, z, ZM).start()
        if c in DIRECT:
            a_r(c, 5, xh, z, Z2).start()

    def C1(c):
        a_c(c, 7, y, xl, XL).start()
        a_c(c, 8, y, xl, YP).start()
        a_c(c, 9, y, xl, YM).start()
        if c in DIRECT:
            a_c(c, 12, y, xl, Y2).start()

    def R2(c):
        a_r(c, 0, 1 - xh, z, XH).wait_recv()
        a_r(c, 3, 1 - xh, z, ZP).start()
        a_r(c, 4, 1 - xh, z, ZM).start()
        if c in DIRECT:
            a_r(c, 6, 1 - xh, z, Z2).start()

    def C2(c):
        a_c(c, 7, y, 1 - xl, XL).wait_recv()
        a_c(c, 10, y, 1 - xl, YP).start()
        a_c(c, 11, y, 1 - xl, YM).start()
        if c in DIRECT:
            a_c(c, 13, y, 1 - xl, Y2).start()

    def R3a(c):
        a_r(c, 0, xh, zp, ZP).wait_recv()
        a_r(c, 5, xh, zp, ZM).start()

    def R3b(c):
        a_r(c, 0, 1 - xh, zm, ZM).wait_recv()
        a_r(c, 6, 1 - xh, zm, ZP).start()

    def C3a(c):
        a_c(c, 7, yp, xl, YP).wait_recv()
        a_c(c, 12, yp, xl, YM).start()

    def C3b(c):
        a_c(c, 7, ym, 1 - xl, YM).wait_recv()
        a_c(c, 13, ym, 1 - xl, YP).start()

    def R4(c):
        if c in DIRECT:
            a_r(c, 0, xh, zp, ZP).wait_recv()
            a_r(c, 0, 1 - xh, zm, ZM).wait_recv()
        for h, q in ((xh, zm), (1 - xh, zp), (xh, z2), (1 - xh, z2)):
            a_r(c, 0, h, q, ZP).wait_recv()
        a_half(c, core).start()

    def C4(c):
        if c in DIRECT:
            a_c(c, 7, yp, xl, YP).wait_recv()
            a_c(c, 7, ym, 1 - xl, YM).wait_recv()
        for q, l in ((ym, xl), (yp, 1 - xl), (y2, xl), (y2, 1 - xl)):
            a_c(c, 7, q, l, YP).wait_recv()

    def R5(c):
        a_half(c, 1 - core).wait_recv()

    def G1(c):
        g_ref[0] = gather(x_ref, c, core * HALF, hot_ref)
        g_ref[1] = jnp.zeros((FEAT, CAP), F32)

    def G2(c):
        def step(kind, carry):
            start = (1 - kind) * (1 - core) * HALF + kind * RROWS
            g_ref[kind] = g_ref[kind] + gather(x_ref, c, start, hot_ref)
            return carry

        lax.fori_loop(0, 2, step, 0)

    def V(c):
        if c == 0:
            for load in loads:
                load.wait()
        multiply(k_ref, g_ref, part_ref)

    def T(c):
        for kind in range(2):
            p = jnp.transpose(g_ref[kind])
            hi = p.astype(BF16)
            pt_ref[kind, :, :FEAT] = hi
            pt_ref[kind, :, FEAT:] = (p - hi.astype(F32)).astype(BF16)

    def sent(c):
        b_half(c).wait_send()
        for n in range(7):
            out_r(c, n).wait_send()
            out_c(c, n).wait_send()

    def S1(c):
        if c >= 2:
            sent(c - 2)
            pl.semaphore_wait(free_sem, 1)
        scatter(pt_ref, 0, (1 - core) * HALF, hot_ref, p_ref, c % 2)
        b_half(c).start()

    def S2(c):
        scatter(pt_ref, 1, RROWS, hot_ref, p_ref, c % 2)
        for n in range(4):
            out_c(c, n).start()

    def S3(c):
        scatter(pt_ref, 0, core * HALF, hot_ref, p_ref, c % 2)

    def D2(c):
        b_half(c).wait_recv()
        p_ref[c % 2, half(core), :] = p_ref[c % 2, half(core), :] + half_ref[c % 2]
        if c + 2 < CHUNKS:
            pl.semaphore_signal(free_sem, inc=1, device_id=SIB, device_id_type=MESH)
        for n in range(4):
            out_r(c, n).start()

    def E2a(c):
        out_c(c, 0).wait_recv()
        add(c, cstrip(yp, xl), cb_ref, 0)
        out_c(c, 4).start()

    def E2b(c):
        out_c(c, 1).wait_recv()
        add(c, cstrip(ym, 1 - xl), cb_ref, 1)
        out_c(c, 5).start()

    def D3a(c):
        out_r(c, 0).wait_recv()
        add(c, rstrip(xh, zp), rb_ref, 0)
        out_r(c, 4).start()

    def D3b(c):
        out_r(c, 1).wait_recv()
        add(c, rstrip(1 - xh, zm), rb_ref, 1)
        out_r(c, 5).start()

    def E3(c):
        for n in (2, 5):
            out_c(c, n).wait_recv()
        add(c, cstrip(y, 1 - xl), cb_ref, 2, 5)
        out_c(c, 6).start()

    def D3(c):
        for n in (2, 5):
            out_r(c, n).wait_recv()
        add(c, rstrip(1 - xh, z), rb_ref, 2, 5)
        out_r(c, 6).start()

    def E4(c):
        for n in (3, 4):
            out_c(c, n).wait_recv()
        add(c, cstrip(y, xl), cb_ref, 3, 4)

    def D4(c):
        for n in (3, 4):
            out_r(c, n).wait_recv()
        add(c, rstrip(xh, z), rb_ref, 3, 4)

    def F(c):
        out_r(c, 6).wait_recv()
        out_c(c, 6).wait_recv()
        total = p_ref[c % 2, rstrip(xh, z), :] + rb_ref[c, 6]
        total = total + (p_ref[c % 2, cstrip(y, xl), :] + cb_ref[c, 6])
        total = jnp.transpose(total)
        for v in range(VC):
            for h in range(2):
                res_ref[h, pl.ds(c * VC + v, B, stride=NV), :] = total[
                    v * B : (v + 1) * B, h * LANES : (h + 1) * LANES
                ]

    steps = dict(R1=R1, C1=C1, R2=R2, C2=C2, R3a=R3a, R3b=R3b, C3a=C3a, C3b=C3b, R4=R4, C4=C4)
    steps.update(R5=R5, G1=G1, G2=G2, V=V, T=T, S1=S1, S2=S2, S3=S3, D2=D2, E2a=E2a, E2b=E2b)
    steps.update(D3a=D3a, D3b=D3b, E3=E3, D3=D3, E4=E4, D4=D4, F=F)
    steps.update(H=H)
    for step in ORDER:
        name, c = step.split(".")
        steps[name](int(c))

    results = [
        pltpu.make_async_copy(
            res_ref.at[h], out_ref.at[:, h * LANES : (h + 1) * LANES], v_sem.at[h]
        )
        for h in range(2)
    ]
    for store in results:
        store.start()
    for c in range(CHUNKS):
        for n in range(7):
            a_r(c, n, xh, z, XH).wait_send()
            a_c(c, 7 + n, y, xl, XL).wait_send()
        a_half(c, core).wait_send()
    for c in range(max(0, CHUNKS - 2), CHUNKS):
        sent(c)
    for store in results:
        store.wait()


def body(vectors, blocks, blk_row, blk_col, live_counts):
    vmem = pl.BlockSpec(memory_space=pltpu.VMEM)
    hbm = pl.BlockSpec(memory_space=pl.ANY)
    dma = pltpu.SemaphoreType.DMA
    return pl.pallas_call(
        kernel,
        out_shape=jax.ShapeDtypeStruct((B * NV, SB), F32),
        in_specs=[hbm, hbm, vmem, vmem, pl.BlockSpec(memory_space=pltpu.SMEM)],
        out_specs=hbm,
        scratch_shapes=[
            pltpu.VMEM((GROUPS, B * B, LANES), F32),
            pltpu.VMEM((CHUNKS, FEAT, ROWS), F32),
            pltpu.VMEM((ROWS, CAP), BF16),
            pltpu.VMEM((2, ROWS, FEAT), F32),
            pltpu.VMEM((2, HALF, FEAT), F32),
            pltpu.VMEM((CHUNKS, 7, SB, FEAT), F32),
            pltpu.VMEM((CHUNKS, 7, SB, FEAT), F32),
            pltpu.VMEM((2, FEAT, CAP), F32),
            pltpu.VMEM((2, CAP, 2 * FEAT), BF16),
            pltpu.VMEM((2, B * NV, LANES), F32),
            pltpu.VMEM((2, B * NV, LANES), F32),
            dma((GROUPS,)),
            dma((2,)),
            dma((CHUNKS, 15)),
            dma((CHUNKS, 9)),
            dma((CHUNKS, 8)),
            dma((CHUNKS, 15)),
            dma((CHUNKS, 8)),
            dma((CHUNKS, 7)),
            pltpu.SemaphoreType.REGULAR,
        ],
        compiler_params=pltpu.CompilerParams(
            collective_id=0, has_side_effects=True, vmem_limit_bytes=63 * 2**20
        ),
        name="block_product",
    )(vectors, blocks, blk_row.reshape(GROUPS, LANES), blk_col.reshape(GROUPS, LANES), live_counts)


def solution(mesh):
    return jax.shard_map(
        body,
        mesh=mesh,
        in_specs=(
            P(None, ("row", "col")),
            P(None, ("row", "col")),
            P(("row", "col")),
            P(("row", "col")),
            P(("row", "col")),
        ),
        out_specs=P(None, ("row", "col")),
        check_vma=False,
    )
```

time: 628 us -> 109 us (0.17)
  local copies, waits for them, and re-layouts: 194 us -> 1.87 us
  waiting for transfers between devices: 185 us -> 0 us
  other arithmetic: 123 us -> 0 us
  matrix products: 109 us -> 0 us
  Pallas kernels: 0 us -> 107 us
  between operations: 13.1 us -> 0.66 us
    dot_general x16 -> x0, matrix products: 109 us -> none  [the longest x8 66.4 us: plain_add(): jnp.einsum('ijg,jvg->ivg', block_tile, source, precision=lax.Precision.HI...]
    scatter-add x16 -> x0, other arithmetic: 107 us -> none  [the longest x8 63.1 us: plain_add(): row_total.at[:, rows_here]]
    pallas_call x0 -> x1, Pallas kernels: none -> 107 us  [body(): pl.pallas_call(kernel, out_shape=jax.ShapeDtypeStruct((B * NV, SB), F32),...]
    all_gather x2 -> x0, waiting for transfers between devices: 92.1 us -> none  [the longest x1 92.1 us: body(): x_cols = lax.all_gather(vectors, 'row', axis=1, tiled=True)]
    reduce_scatter x2 -> x0, waiting for transfers between devices: 92 us -> none  [the longest x1 91.9 us: body(): lax.psum_scatter(col_total, 'row', scatter_dimension=1, tiled=True)]
    reshape x16 -> x0, local copies, waits for them, and re-layouts: 72.1 us -> none  [fetch_slots(): lax.dynamic_slice_in_dim(blocks, offset, group_size, 1)]
    gather x32 -> x0, local copies, waits for them, and re-layouts: 60.8 us -> none  [the longest x16 35.3 us: mirror_add(): source = jnp.take(x_rows, rows_here, axis=1).reshape(B, NV, group_size)]
    dynamic_slice x16 -> x0, local copies, waits for them, and re-layouts: 27.9 us -> none  [fetch_slots(): lax.dynamic_slice_in_dim(blocks, offset, group_size, 1)]
  transfers between devices with their start and end apart: 4 -> 0, of which waited for: 2 -> 0; matrix products, arithmetic and copies ran while one was open for 67% -> 0% of each run, Pallas kernels for 0% -> 0%
where the time goes in v1:
time: 109 us
  Pallas kernels  107 us (98%)
  local copies, waits for them, and re-layouts  1.87 us (2%)
    pallas_call x1, Pallas kernels, body(): pl.pallas_call(kernel, out_shape=jax.ShapeDtypeStruct((B * NV, SB), F32),...  107 us

profile of v1, /device:TPU:0, one launch (start us, length us, event | category | flops | bytes accessed | tf_op | source)
XLA Modules:
  0.0 109.2 jit_solution(2768315352074642777)
XLA Ops:
  0.7 106.6 %block_product.1 = f32[512,256]{1,0:T(8,128)} custom-call(f32[512,256]{1,0:T(8,128)} %vec_ref.1, f32[4096,1024]{1,0:T(8,128)} %blk_ref.1, s32[8,128]{1,0:T(8,128)} %bitcast.2, s32[8,128]{1,0:T(8,128)} %bitcast.3, s32[1]{0:T(128)S(6)} %copy.7.live_ref), custom_call_target="tpu_custom_call" | custom-call | tf_op jit(solution)/shard_map/block_product/pallas_call | solution.py:496
  107.3 1.9 %copy.8 = f32[512,256]{1,0:T(8,128)} copy(f32[512,256]{1,0:T(8,128)} %block_product.1) | data formatting | bytes 1048576

commit v2 on v1

--- a/solution.py
+++ b/solution.py
@@ -29,7 +29,7 @@
 DIRECT = ()
 
 ORDER = (
-    "R1.0", "C1.0", "R1.1", "R2.0", "C1.2", "C2.0", "C1.1", "R3a.0", "H.0", "R3b.0", "R2.1",
+    "R1.0", "C1.0", "R1.1", "R2.0", "C1.2", "C2.0", "C1.1", "R3a.0", "R3b.0", "R2.1",
     "C3a.0", "R1.2", "C3b.0", "R1.3", "C2.2", "R3a.1", "C3a.1", "R4.0", "C2.1", "C1.3", "G1.0",
     "R3b.1", "R5.0", "C3a.2", "R2.2", "C4.0", "G2.0", "V.0", "T.0", "R3a.3", "C3b.1", "S1.0",
     "R3a.2", "R4.1", "C2.3", "R2.3", "G1.1", "S3.0", "S2.0", "R3b.2", "R5.1", "C3b.2", "D2.0",
@@ -221,6 +221,9 @@
                     lanes = pl.ds(pl.multiple_of(p * SB + h * LANES, LANES), LANES)
                     x_ref[c, v * B : (v + 1) * B, lanes] = x
 
+    r_place, c_place = places(brow_ref[...], bcol_ref[...], live_ref[0])
+    one_hots(r_place, 0, RROWS, hot_ref)
+    one_hots(c_place, RROWS, CROWS, hot_ref)
     pl.semaphore_wait(barrier, 9)
 
     def copy(src, dst, send, recv, peer):
@@ -287,11 +290,6 @@
         )
         return b_c(c, n, *to[n])
 
-    def H(c):
-        r_place, c_place = places(brow_ref[...], bcol_ref[...], live_ref[0])
-        one_hots(r_place, 0, RROWS, hot_ref)
-        one_hots(c_place, RROWS, CROWS, hot_ref)
-
     def R1(c):
         a_r(c, 0, xh, z, XH).start()
         a_r(c, 1, xh, z, ZP).start()
@@ -465,7 +463,6 @@
     steps = dict(R1=R1, C1=C1, R2=R2, C2=C2, R3a=R3a, R3b=R3b, C3a=C3a, C3b=C3b, R4=R4, C4=C4)
     steps.update(R5=R5, G1=G1, G2=G2, V=V, T=T, S1=S1, S2=S2, S3=S3, D2=D2, E2a=E2a, E2b=E2b)
     steps.update(D3a=D3a, D3b=D3b, E3=E3, D3=D3, E4=E4, D4=D4, F=F)
-    steps.update(H=H)
     for step in ORDER:
         name, c = step.split(".")
         steps[name](int(c))

time: 109 us -> 113 us (1.037)
  Pallas kernels: 107 us -> 110 us
    pallas_call x1, Pallas kernels: 107 us -> 110 us  [body(): pl.pallas_call(kernel, out_shape=jax.ShapeDtypeStruct((B * NV, SB), F32),...]
where the time goes in v2:
time: 113 us
  Pallas kernels  110 us (97%)
  local copies, waits for them, and re-layouts  1.87 us (2%)
    pallas_call x1, Pallas kernels, body(): pl.pallas_call(kernel, out_shape=jax.ShapeDtypeStruct((B * NV, SB), F32),...  110 us

profile of v2, /device:TPU:0, one launch (start us, length us, event | category | flops | bytes accessed | tf_op | source)
XLA Modules:
  0.0 112.6 jit_solution(11855589082438201614)
XLA Ops:
  0.7 110.1 %block_product.1 = f32[512,256]{1,0:T(8,128)} custom-call(f32[512,256]{1,0:T(8,128)} %vec_ref.1, f32[4096,1024]{1,0:T(8,128)} %blk_ref.1, s32[8,128]{1,0:T(8,128)} %bitcast.2, s32[8,128]{1,0:T(8,128)} %bitcast.3, s32[1]{0:T(128)S(6)} %copy.7.live_ref), custom_call_target="tpu_custom_call" | custom-call | tf_op jit(solution)/shard_map/block_product/pallas_call | solution.py:493
  110.7 1.9 %copy.8 = f32[512,256]{1,0:T(8,128)} copy(f32[512,256]{1,0:T(8,128)} %block_product.1) | data formatting | bytes 1048576
